TPU v7x, 512 devices: a whole 4x4x16 slice. The times are simulated.
512 devices in a mesh: section: 32 (over z, x_lo), tensor: 16 (over y, x_hi, core).
Axes of the slice: x: 4 (x_hi: 2, x_lo: 2; x = x_hi * 2 + x_lo), y: 4, z: 16, core: 2. Of those that a mesh axis runs over, the one named last changes fastest.
Arguments:
- old_query: bfloat16 [32, 4096, 4096], P('section', 'tensor'), may hold values from -0.09375 to 0.09375
- old_key: bfloat16 [32, 4096, 1024], P('section', 'tensor'), may hold values from -0.09375 to 0.09375
- old_value: bfloat16 [32, 4096, 1024], P('section', 'tensor'), may hold values from -0.09375 to 0.09375
- depth_mix: float32 [32], replicated, may hold values from -1 to 1
- width_query: bfloat16 [8192, 4096], P('section', 'tensor'), may hold values from -0.09375 to 0.09375
- width_kv: bfloat16 [1024, 1024], P('section', 'tensor'), may hold values from -0.1875 to 0.1875
- width_stream: bfloat16 [8192, 4096], P('tensor', 'section'), may hold values from -0.0625 to 0.0625
- hidden: bfloat16 [2048, 8192], P('section', 'tensor'), may hold values from -8 to 8
Outputs:
- grown_query: bfloat16 [8192, 8192], P('tensor', 'section')
- grown_key: bfloat16 [8192, 1024], P('tensor', 'section')
- grown_value: bfloat16 [8192, 1024], P('tensor', 'section')
- attended: bfloat16 [2048, 8192], P('tensor', 'section')
All inputs are finite; a program needn't handle non-finite values.
Results may differ from a plain program's by a relative error of at most 0.034.
Values may be sent and summed in bfloat16 or wider, within the bound.
No kernel may reach another device: no remote copies, remote signals or barrier semaphores. Data moves between devices by JAX's collectives and lax.ppermute only.
A program may use at most 64 MiB of HBM per device.

v0:
```python
import math

import jax
import jax.numpy as jnp
from jax import lax
from jax.sharding import PartitionSpec as P

HD = 128
KVH = 8


def contract_last(left_side, right_side):
    return lax.dot_general(
        left_side, right_side, (((1,), (1,)), ((), ())), preferred_element_type=jnp.float32
    )


def mix_layers(depth_mix, stacked):
    flattened = stacked.reshape(stacked.shape[0], -1)
    mixed = jnp.dot(
        depth_mix, flattened, precision=lax.Precision.HIGHEST, preferred_element_type=jnp.float32
    )
    return mixed.reshape(stacked.shape[1:]).astype(jnp.bfloat16)


def pick_heads(wide, kv_ids):
    row_count = wide.shape[0]
    grouped = wide.reshape(row_count, KVH, HD)
    chosen = jnp.take(grouped, kv_ids, axis=1)
    return chosen.reshape(row_count, kv_ids.shape[0] * HD)


def per_device(
    old_query, old_key, old_value, depth_mix, width_query, width_kv, width_stream, hidden
):
    section_index = lax.axis_index("section")
    tensor_index = lax.axis_index("tensor")
    tensor_count = lax.axis_size("tensor")
    moved_query, moved_key, moved_value = (
        lax.all_to_all(old_query, "section", split_axis=2, concat_axis=0, tiled=True),
        lax.all_to_all(old_key, "section", split_axis=2, concat_axis=0, tiled=True),
        lax.all_to_all(old_value, "section", split_axis=2, concat_axis=0, tiled=True),
    )
    part_query = mix_layers(depth_mix, moved_query)
    part_key = mix_layers(depth_mix, moved_key)
    part_value = mix_layers(depth_mix, moved_value)
    mixed_query, mixed_key, mixed_value = (
        lax.all_gather(part_query, "section", axis=1, tiled=True),
        lax.all_gather(part_key, "section", axis=1, tiled=True),
        lax.all_gather(part_value, "section", axis=1, tiled=True),
    )
    query_width, kv_width = (
        lax.all_gather(width_query, "tensor", axis=1, tiled=True),
        lax.all_gather(width_kv, "tensor", axis=1, tiled=True),
    )
    expanded_query = contract_last(mixed_query, query_width).astype(jnp.bfloat16)
    expanded_key = contract_last(mixed_key, kv_width).astype(jnp.bfloat16)
    expanded_value = contract_last(mixed_value, kv_width).astype(jnp.bfloat16)
    whole_query, whole_key, whole_value = (
        lax.all_gather(expanded_query, "tensor", axis=0, tiled=True),
        lax.all_gather(expanded_key, "tensor", axis=0, tiled=True),
        lax.all_gather(expanded_value, "tensor", axis=0, tiled=True),
    )
    fragment = lax.all_gather(width_stream, "section", axis=1, tiled=True)

    def product_of(whole):
        return jnp.dot(fragment, whole, preferred_element_type=jnp.float32)

    sum_query = product_of(whole_query)
    sum_key = product_of(whole_key)
    sum_value = product_of(whole_value)
    grown_query = sum_query.astype(jnp.bfloat16)
    grown_key = sum_key.astype(jnp.bfloat16)
    grown_value = sum_value.astype(jnp.bfloat16)
    all_hidden = lax.all_gather(hidden, "section", axis=0, tiled=True)
    token_count = all_hidden.shape[0]
    block_rows = token_count // tensor_count
    query_cols = grown_query.shape[1]
    heads_here = query_cols // HD
    head_ids = section_index * heads_here + jnp.arange(heads_here, dtype=jnp.int32)
    kv_ids = head_ids % KVH
    joined = jnp.concatenate([grown_query, grown_key, grown_value], axis=1)
    summed = lax.psum_scatter(
        jnp.dot(all_hidden, joined, preferred_element_type=jnp.float32),
        "tensor",
        scatter_dimension=0,
        tiled=True,
    )
    kv_cols = (summed.shape[1] - query_cols) // 2
    queries = summed[:, :query_cols].astype(jnp.bfloat16)
    key_part = summed[:, query_cols : query_cols + kv_cols].astype(jnp.bfloat16)
    value_part = summed[:, query_cols + kv_cols :].astype(jnp.bfloat16)
    key_wide, value_wide = (
        lax.all_gather(key_part, "section", axis=1, tiled=True),
        lax.all_gather(value_part, "section", axis=1, tiled=True),
    )
    key_here = pick_heads(key_wide, kv_ids)
    value_here = pick_heads(value_wide, kv_ids)
    key_rows, value_rows = (
        lax.all_gather(key_here, "tensor", axis=0, tiled=True),
        lax.all_gather(value_here, "tensor", axis=0, tiled=True),
    )
    query_heads = queries.reshape(block_rows, heads_here, HD)
    key_heads = key_rows.reshape(token_count, heads_here, HD)
    value_heads = value_rows.reshape(token_count, heads_here, HD)
    scores = jnp.einsum(
        "qhd,khd->hqk", query_heads, key_heads, preferred_element_type=jnp.float32
    ) * (1.0 / math.sqrt(HD))
    query_position = tensor_index * block_rows + lax.broadcasted_iota(jnp.int32, (block_rows, 1), 0)
    key_position = lax.broadcasted_iota(jnp.int32, (1, token_count), 1)
    scores = jnp.where((key_position <= query_position)[None], scores, -jnp.inf)
    row_max = jnp.max(scores, axis=2, keepdims=True)
    weights = jnp.exp(scores - row_max)
    denominator = jnp.sum(weights, axis=2, keepdims=True)
    probs = weights.astype(jnp.bfloat16)
    mixed_out = (
        jnp.einsum("hqk,khd->hqd", probs, value_heads, preferred_element_type=jnp.float32)
        / denominator
    )
    attended = (
        jnp.transpose(mixed_out, (1, 0, 2))
        .reshape(block_rows, heads_here * HD)
        .astype(jnp.bfloat16)
    )
    return (grown_query, grown_key, grown_value, attended)


def solution(mesh):
    placed = (
        P("section", "tensor", None),
        P("section", "tensor", None),
        P("section", "tensor", None),
        P(),
        P("section", "tensor"),
        P("section", "tensor"),
        P("tensor", "section"),
        P("section", "tensor"),
    )
    return jax.shard_map(
        per_device,
        mesh=mesh,
        in_specs=placed,
        out_specs=(
            P("tensor", "section"),
            P("tensor", "section"),
            P("tensor", "section"),
            P("tensor", "section"),
        ),
        check_vma=False,
    )
```

profile of v0, /device:TPU:1, one launch (start us, length us, event | category | flops | bytes accessed | tf_op | source)
XLA Modules:
  0.0 1042.3 jit_solution(12632971732343186485)
XLA Ops:
  7.2 10.0 copy.36
  17.7 21.6 %reduce.4 = bf16[4096,256]{1,0:T(8,128)(2,1)S(1)} reduce(bf16[4096,1,256]{2,1,0:T(2,128)(2,1)} %bitcast.101, bf16[]{:T(256)} %broadcast.72), dimensions={1}, to_apply=%bitcast.75.reduce_sub_computation | reduce | bytes 4194306
  41.3 17.0 %all-to-all-start = ((bf16[32,2,16384]{2,1,0:T(2,128)(2,1)}), bf16[32,2,16384]{2,1,0:T(2,128)(2,1)S(1)}, u32[]{:S(2)}, u32[]{:S(2)}) async-start(bf16[32,2,16384]{2,1,0:T(2,128)(2,1)} %reshape.120), calls=%async_computation | async-start | bytes 4194304 | tf_op jit(solution)/shard_map/all_to_all | solution.py:40
  59.1 95.6 %all-to-all-done = bf16[32,2,16384]{2,1,0:T(2,128)(2,1)S(1)} async-done(((bf16[32,2,16384]{2,1,0:T(2,128)(2,1)}), bf16[32,2,16384]{2,1,0:T(2,128)(2,1)S(1)}, u32[]{:S(2)}, u32[]{:S(2)}) %all-to-all-start) | async-done | bytes 2097184 | tf_op jit(solution)/shard_map/all_to_all | solution.py:40
  154.7 6.7 reshape.121
  161.4 2.5 copy.61
  164.0 2.9 copy.37
  166.9 3.4 fusion.1
  171.8 109.2 %all-gather.9.cloned.1.call-done = bf16[256,4096]{1,0:T(8,128)(2,1)} async-done(((bf16[256,128]{1,0:T(8,128)(2,1)}), bf16[256,4096]{1,0:T(8,128)(2,1)}) %all-gather.9.cloned.1.call-update) | async-done | bytes 2097168 | tf_op jit(solution)/shard_map/all_gather | solution.py:48
  281.0 3.6 convolution_convert_fusion.1
  285.5 3.9 reduce.5
  290.4 6.0 all-to-all-start.2
  297.3 3.8 reduce.6
  302.0 16.1 %all-to-all-done.2 = bf16[32,2,4096]{2,1,0:T(2,128)(2,1)S(1)} async-done(((bf16[32,2,4096]{2,1,0:T(2,128)(2,1)}), bf16[32,2,4096]{2,1,0:T(2,128)(2,1)S(1)}, u32[]{:S(2)}, u32[]{:S(2)}) %all-to-all-start.2) | async-done | bytes 524320 | tf_op jit(solution)/shard_map/all_to_all | solution.py:42
  318.1 3.9 all-to-all-start.1
  322.6 67.5 %all-gather = bf16[16,64,32]{1,2,0:T(8,128)(2,1)S(1)} all-gather(bf16[1,64,32]{1,2,0:T(8,128)(2,1)S(1)} %bitcast.122), channel_id=1, replica_groups=mesh['section'=32,'tensor'=16] {'tensor'}, dimensions={0}, use_global_device_ids=true | all-gather | bytes 69632 | tf_op jit(solution)/shard_map/all_gather | solution.py:54
  394.3 2.6 dot_general.63
  400.9 2.6 dot_general.58
  403.5 2.8 multiply_reduce_fusion
  406.4 58.4 %all_gather.46 = bf16[256,1024]{0,1:T(8,128)(2,1)S(1)} all-gather(bf16[256,32]{0,1:T(8,128)(2,1)S(1)} %copy.53), channel_id=1, replica_groups=mesh['section'=32,'tensor'=16] {'section'}, dimensions={1}, use_global_device_ids=true | all-gather | bytes 540672 | tf_op jit(solution)/shard_map/all_gather | solution.py:49
  465.0 32.4 %all_gather.48 = bf16[4096,32]{0,1:T(8,128)(2,1)S(1)} all-gather(bf16[256,32]{0,1:T(8,128)(2,1)S(1)} %convolution_convert_fusion.5), channel_id=1, replica_groups=mesh['section'=32,'tensor'=16] {'tensor'}, dimensions={0}, use_global_device_ids=true | all-gather | bytes 278528 | tf_op jit(solution)/shard_map/all_gather | solution.py:61
  497.5 47.9 %all_gather.49 = bf16[256,1024]{0,1:T(8,128)(2,1)S(1)} all-gather(bf16[256,32]{0,1:T(8,128)(2,1)S(1)} %copy.58), channel_id=1, replica_groups=mesh['section'=32,'tensor'=16] {'section'}, dimensions={1}, use_global_device_ids=true | all-gather | bytes 540672 | tf_op jit(solution)/shard_map/all_gather | solution.py:50
  545.6 36.0 %all_gather.50 = bf16[4096,32]{0,1:T(8,128)(2,1)S(1)} all-gather(bf16[256,32]{0,1:T(8,128)(2,1)S(1)} %convolution_convert_fusion.4), channel_id=1, replica_groups=mesh['section'=32,'tensor'=16] {'tensor'}, dimensions={0}, use_global_device_ids=true | all-gather | bytes 278528 | tf_op jit(solution)/shard_map/all_gather | solution.py:62
  581.6 3.7 fusion.9
  586.7 4.1 fusion.6
  590.9 79.0 %all-gather.17.cloned.1.call-done = bf16[2048,512]{1,0:T(8,128)(2,1)} async-done(((bf16[64,512]{1,0:T(8,128)(2,1)}), bf16[2048,512]{1,0:T(8,128)(2,1)}) %all-gather.17.cloned.1.call-update) | async-done | bytes 2097168 | tf_op jit(solution)/shard_map/all_gather | solution.py:75
  669.8 4.0 convolution_bitcast_fusion
  673.9 114.0 %reduce-scatter.2.cloned.1.call-done = f32[128,320]{0,1:T(8,128)} async-done(((f32[2048,320]{0,1:T(8,128)}), f32[128,320]{0,1:T(8,128)}) %reduce-scatter.2.cloned.1.call-update) | async-done | bytes 163856 | tf_op jit(solution)/shard_map/reduce_scatter | solution.py:83
  788.9 49.9 %all_gather.52 = bf16[128,1024]{0,1:T(8,128)(2,1)S(1)} all-gather(bf16[128,32]{0,1:T(8,128)(2,1)S(1)} %get-tuple-element.23), channel_id=1, replica_groups=mesh['section'=32,'tensor'=16] {'section'}, dimensions={1}, use_global_device_ids=true | all-gather | bytes 270336 | tf_op jit(solution)/shard_map/all_gather | solution.py:94
  838.8 45.9 %all_gather.54 = bf16[128,1024]{0,1:T(8,128)(2,1)S(1)} all-gather(bf16[128,32]{0,1:T(8,128)(2,1)S(1)} %get-tuple-element.24), channel_id=1, replica_groups=mesh['section'=32,'tensor'=16] {'section'}, dimensions={1}, use_global_device_ids=true | all-gather | bytes 270336 | tf_op jit(solution)/shard_map/all_gather | solution.py:95
  888.4 83.1 %all-gather.19.cloned.1.call-done = bf16[2048,256]{0,1:T(8,128)(2,1)} async-done(((bf16[128,256]{0,1:T(8,128)(2,1)}), bf16[2048,256]{0,1:T(8,128)(2,1)}) %all-gather.19.cloned.1.call-update) | async-done | bytes 1048592 | tf_op jit(solution)/shard_map/all_gather | solution.py:100
  973.9 59.1 %all-gather.21.cloned.1.call-done = bf16[2048,256]{0,1:T(8,128)(2,1)} async-done(((bf16[128,256]{0,1:T(8,128)(2,1)}), bf16[2048,256]{0,1:T(8,128)(2,1)}) %all-gather.21.cloned.1.call-update) | async-done | bytes 1048592 | tf_op jit(solution)/shard_map/all_gather | solution.py:101
  (74 shorter events, 28.5 us)
Async XLA Ops:
  41.3 113.3 %all-to-all-start = ((bf16[32,2,16384]{2,1,0:T(2,128)(2,1)}), bf16[32,2,16384]{2,1,0:T(2,128)(2,1)S(1)}, u32[]{:S(2)}, u32[]{:S(2)}) async-start(bf16[32,2,16384]{2,1,0:T(2,128)(2,1)} %reshape.120), calls=%async_computation | async-start | bytes 4194304 | tf_op jit(solution)/shard_map/all_to_all | solution.py:40
  58.3 113.5 %all-gather.11.cloned.1.call-start = ((), (), s32[]{:S(2)}) async-start(), calls=%async_computation.5 | async-start | bytes 2228224 | tf_op jit(solution)/shard_map/all_gather | solution.py:53
  59.0 222.0 %all-gather.9.cloned.1.call-start = ((), (), s32[]{:S(2)}) async-start(), calls=%async_computation.4 | async-start | bytes 2162688 | tf_op jit(solution)/shard_map/all_gather | solution.py:48
  164.0 2.9 copy-start.7
  171.0 410.6 %all-gather.15.cloned.1.call-start = ((), (), s32[]{:S(2)}) async-start(), calls=%async_computation.7 | async-start | bytes 4325376 | tf_op jit(solution)/shard_map/all_gather | solution.py:64
  171.7 113.0 %copy-start.2 = (bf16[1,256,1024]{2,1,0:T(8,128)(2,1)S(1)}, bf16[1,256,1024]{2,1,0:T(8,128)(2,1)}, u32[]{:S(2)}) copy-start(bf16[1,256,1024]{2,1,0:T(8,128)(2,1)} %param.12) | copy-start | bytes 1572868
  171.7 415.0 %all-gather.13.cloned.1.call-start = ((), (), s32[]{:S(2)}) async-start(), calls=%async_computation.6 | async-start | bytes 2228224 | tf_op jit(solution)/shard_map/all_gather | solution.py:60
  285.5 10.8 %copy-start.3 = (bf16[1,256,1024]{2,1,0:T(8,128)(2,1)S(1)}, bf16[1,256,1024]{2,1,0:T(8,128)(2,1)}, u32[]{:S(2)}) copy-start(bf16[1,256,1024]{2,1,0:T(8,128)(2,1)} %param.11) | copy-start | bytes 1572868
  290.4 27.7 %all-to-all-start.2 = ((bf16[32,2,4096]{2,1,0:T(2,128)(2,1)}), bf16[32,2,4096]{2,1,0:T(2,128)(2,1)S(1)}, u32[]{:S(2)}, u32[]{:S(2)}) async-start(bf16[32,2,4096]{2,1,0:T(2,128)(2,1)} %reshape.122), calls=%async_computation.2 | async-start | bytes 1048576 | tf_op jit(solution)/shard_map/all_to_all | solution.py:42
  297.2 25.4 %copy-start.6 = (bf16[32,64]{1,0:T(8,128)(2,1)S(1)}, bf16[32,64]{1,0:T(8,128)(2,1)}, u32[]{:S(2)}) copy-start(bf16[32,64]{1,0:T(8,128)(2,1)} %param.15) | copy-start | bytes 12292
  318.1 78.8 %all-to-all-start.1 = ((bf16[32,2,4096]{2,1,0:T(2,128)(2,1)}), bf16[32,2,4096]{2,1,0:T(2,128)(2,1)S(1)}, u32[]{:S(2)}, u32[]{:S(2)}) async-start(bf16[32,2,4096]{2,1,0:T(2,128)(2,1)} %reshape.124), calls=%async_computation.1 | async-start | bytes 1048576 | tf_op jit(solution)/shard_map/all_to_all | solution.py:41
  322.0 347.9 %all-gather.17.cloned.1.call-start = ((), (), s32[]{:S(2)}) async-start(), calls=%async_computation.8 | async-start | bytes 2162688 | tf_op jit(solution)/shard_map/all_gather | solution.py:75
  322.6 465.4 %reduce-scatter.2.cloned.1.call-start = ((), (), s32[]{:S(2)}) async-start(), calls=%async_computation.9 | async-start | bytes 2785280 | tf_op jit(solution)/shard_map/reduce_scatter | solution.py:83
  400.8 2.6 copy-start.1
  581.6 3.7 copy-start
  585.3 84.5 %copy-start.4 = (bf16[512,32]{0,1:T(8,128)(2,1)}, bf16[512,32]{0,1:T(8,128)(2,1)S(1)}, u32[]{:S(2)}) copy-start(bf16[512,32]{0,1:T(8,128)(2,1)S(1)} %fusion.9) | copy-start | bytes 98308
  586.7 83.2 %copy-start.5 = (bf16[512,32]{0,1:T(8,128)(2,1)}, bf16[512,32]{0,1:T(8,128)(2,1)S(1)}, u32[]{:S(2)}) copy-start(bf16[512,32]{0,1:T(8,128)(2,1)S(1)} %fusion.10) | copy-start | bytes 98308
  673.8 297.7 %all-gather.19.cloned.1.call-start = ((), (), s32[]{:S(2)}) async-start(), calls=%async_computation.10 | async-start | bytes 1114112 | tf_op jit(solution)/shard_map/all_gather | solution.py:100
  886.5 146.4 %all-gather.21.cloned.1.call-start = ((), (), s32[]{:S(2)}) async-start(), calls=%async_computation.11 | async-start | bytes 1114112 | tf_op jit(solution)/shard_map/all_gather | solution.py:101
Sparse Core Ops, SparseCore 0:
  62.3 65.4 all-gather.10
  171.1 109.8 all-gather.8
  283.0 193.3 all-gather.14
  480.2 75.4 all-gather.12
  557.6 112.1 all-gather.16
  674.6 113.2 reduce-scatter.1
  886.7 84.7 all-gather.18
  974.7 58.1 all-gather.20
where the time goes:
time: 1040 us
  waiting for transfers between devices  559 us (54%)
  blocking collectives  338 us (32%)
  local copies, waits for them, and re-layouts  44.6 us (4%)
  other arithmetic  35 us (3%)
  starting transfers between devices  27.2 us (3%)
  matrix products  24.2 us (2%)
  between operations  14.5 us (1%)
    reduce_scatter x1, waiting for transfers between devices, per_device(): lax.psum_scatter(jnp.dot(all_hidden, joined, preferred_element_type=jnp.f...  114 us
    all_gather x1, waiting for transfers between devices, per_device(): lax.all_gather(part_query, 'section', axis=1, tiled=True)  109 us
    all_to_all x1, waiting for transfers between devices, per_device(): lax.all_to_all(old_query, 'section', split_axis=2, concat_axis=0, tiled=T...  95.6 us
    all_gather x1, waiting for transfers between devices, per_device(): lax.all_gather(key_here, 'tensor', axis=0, tiled=True)  83.1 us
    all_gather x1, waiting for transfers between devices, per_device(): all_hidden = lax.all_gather(hidden, 'section', axis=0, tiled=True)  79 us
    all_gather x1, blocking collectives, per_device(): lax.all_gather(width_kv, 'tensor', axis=1, tiled=True)  67.5 us
    all_gather x1, waiting for transfers between devices, per_device(): lax.all_gather(value_here, 'tensor', axis=0, tiled=True)  59.1 us
    all_gather x1, blocking collectives, per_device(): lax.all_gather(part_key, 'section', axis=1, tiled=True)  58.4 us
  transfers between devices with their start and end apart: 11, of which 7 were waited for; matrix products, arithmetic and copies ran while one was open for 6% of the time, Pallas kernels for 0%

commit v1 on v0

v1 whole, which is shorter than its diff:
```python
import math

import jax
import jax.numpy as jnp
from jax import lax
from jax.experimental import pallas as pl
from jax.experimental.pallas import tpu as pltpu
from jax.sharding import Mesh, PartitionSpec as P

HD = 128
KVH = 8
BF = jnp.bfloat16
F32 = jnp.float32
Z = ("q", "r")
SECTION = ("q", "r", "x")
TENSOR = ("y", "h", "c")
Q, R, X, Y, H, C = 4, 4, 2, 4, 2, 2
ZS, TS = Q * R, Y * H * C


def shift(value, distance):
    return lax.ppermute(value, Z, [(i, (i + distance) % ZS) for i in range(ZS)])


def partner(value, axis, bit=1):
    size = {"x": X, "y": Y, "h": H, "c": C, "r": R}[axis]
    return lax.ppermute(value, axis, [(i, i ^ bit) for i in range(size)])


def pair_up(value, axis, dim, bit=1):
    other = partner(value, axis, bit)
    low = (lax.axis_index(axis) & bit) == 0
    return jnp.concatenate([jnp.where(low, value, other), jnp.where(low, other, value)], axis=dim)


def gather_tensor(value):
    shape = value.shape
    value = pair_up(value[None], "h", 0)
    value = pair_up(value[None], "y", 0, 1)
    value = pair_up(value[None], "y", 0, 2)
    value = pair_up(value.reshape((Y * H, 1) + shape), "c", 1)
    return value.reshape((TS,) + shape)


def gather_blocks(value):
    for axis, bit in (("h", 1), ("y", 1), ("y", 2)):
        value = jnp.stack([value, partner(value, axis, bit)], axis=0)
    shape = value.shape[3:]
    value = value.reshape((Y * H,) + shape)
    return value, partner(value, "c")


def dot(a, b, ca, cb):
    return lax.dot_general(a, b, (((ca,), (cb,)), ((), ())), preferred_element_type=F32)


def in_vmem(count):
    return [pl.BlockSpec(memory_space=pltpu.SMEM)] + [pl.BlockSpec(memory_space=pltpu.VMEM)] * count


def expand_query(index, mixed, own, other, n_q, gap):
    rows = mixed.shape[0]
    count, _, part = own.shape

    def kernel(index_ref, mixed_ref, own_ref, other_ref, out_ref):
        t = index_ref[0]
        low = jnp.zeros((rows, n_q), F32)
        high = jnp.zeros((rows, n_q), F32)
        for i in range(count):
            for bit, ref in ((0, own_ref), (1, other_ref)):
                chunk = t ^ (2 * i + bit)
                left = mixed_ref[:, pl.ds(pl.multiple_of(chunk * part, part), part)]
                low += dot(left, ref[i, :n_q, :], 1, 1)
                high += dot(left, ref[i, gap : gap + n_q, :], 1, 1)
        out_ref[:, :n_q] = low.astype(BF)
        out_ref[:, n_q:] = high.astype(BF)

    return pl.pallas_call(
        kernel,
        out_shape=jax.ShapeDtypeStruct((rows, 2 * n_q), BF),
        in_specs=in_vmem(3),
        out_specs=pl.BlockSpec(memory_space=pltpu.VMEM),
        compiler_params=pltpu.CompilerParams(vmem_limit_bytes=24 << 20),
        cost_estimate=pl.CostEstimate(
            flops=4 * rows * n_q * 2 * count * part,
            bytes_accessed=2 * (mixed.size + own.size + other.size + 2 * rows * n_q),
            transcendentals=0,
        ),
    )(index, mixed, own, other)


def attend(index, queries, own, other):
    rows, width = queries.shape
    heads, count = width // HD, own.shape[0]
    tokens = own.shape[2]
    scale = 1.0 / math.sqrt(HD)
    blocks = [(i, bit) for i in range(count) for bit in (0, 1)]

    def kernel(index_ref, query_ref, own_ref, other_ref, out_ref, scores_ref):
        t = index_ref[0]
        refs = (own_ref, other_ref)
        query_position = t * rows + lax.broadcasted_iota(jnp.int32, (rows, tokens), 0)
        key_offset = lax.broadcasted_iota(jnp.int32, (rows, tokens), 1)
        for head in range(heads):
            at = head * HD
            query = query_ref[:, at : at + HD]
            for n, (i, bit) in enumerate(blocks):
                block = t ^ (2 * i + bit)
                value = dot(query, refs[bit][i, at : at + HD, :], 1, 0) * scale
                seen = block * tokens + key_offset <= query_position
                scores_ref[:, n * tokens : (n + 1) * tokens] = jnp.where(seen, value, -jnp.inf)
            row_max = jnp.max(scores_ref[...], axis=1, keepdims=True)
            denominator = jnp.zeros((rows, 1), F32)
            total = jnp.zeros((rows, HD), F32)
            for n, (i, bit) in enumerate(blocks):
                weights = jnp.exp(scores_ref[:, n * tokens : (n + 1) * tokens] - row_max)
                denominator += jnp.sum(weights, axis=1, keepdims=True)
                value_head = refs[bit][i, width + at : width + at + HD, :]
                total += dot(weights.astype(BF), value_head, 1, 1)
            out_ref[:, at : at + HD] = (total / denominator).astype(BF)

    return pl.pallas_call(
        kernel,
        out_shape=jax.ShapeDtypeStruct((rows, width), BF),
        in_specs=in_vmem(3),
        out_specs=pl.BlockSpec(memory_space=pltpu.VMEM),
        scratch_shapes=[pltpu.VMEM((rows, 2 * count * tokens), F32)],
        compiler_params=pltpu.CompilerParams(vmem_limit_bytes=24 << 20),
        cost_estimate=pl.CostEstimate(
            flops=8 * rows * width * count * tokens,
            bytes_accessed=2 * (own.size + other.size + 2 * rows * width),
            transcendentals=2 * rows * heads * count * tokens,
        ),
    )(index, queries, own, other)


def per_device(
    old_query, old_key, old_value, depth_mix, width_query, width_kv, width_stream, hidden
):
    z = lax.axis_index(Z)
    x = lax.axis_index("x")
    t = lax.axis_index(TENSOR)
    index = t[None].astype(jnp.int32)

    stream = lax.all_gather(width_stream, Z, axis=1, tiled=True)

    old = jnp.concatenate([old_query[0], old_key[0], old_value[0]], axis=1)
    rows, cols = old.shape[0] // X, old.shape[1]
    half = cols // 2
    deep = rows // ZS
    blocks = old.reshape(X, Q, R, deep, cols)

    def weight(offset):
        return lax.dynamic_index_in_dim(depth_mix, ((z + offset) % ZS) * X + x, 0, False)

    def for_class(offset):
        return lax.dynamic_index_in_dim(blocks, (z + offset) % R, 2, False)

    after, before, far, width_query = lax.optimization_barrier(
        (for_class(1), for_class(3), for_class(2), width_query)
    )
    after, before = shift(after, 1), shift(before, -1)
    far_low, far_high = shift(far[..., :half], 2), shift(far[..., half:], -2)
    close = (
        for_class(0).astype(F32) * weight(0)
        + after.astype(F32) * weight(-1)
        + before.astype(F32) * weight(1)
    )
    summed_near = jnp.concatenate(
        [
            close[..., :half] + far_low.astype(F32) * weight(-2),
            close[..., half:] + far_high.astype(F32) * weight(2),
        ],
        axis=-1,
    ).astype(BF)
    keep = lax.dynamic_index_in_dim(summed_near, x, 0, False)
    other = partner(lax.dynamic_index_in_dim(summed_near, 1 - x, 0, False), "x")
    summed = (keep.astype(F32) + other.astype(F32)).astype(BF)
    pieces = lax.all_to_all(summed, "q", 0, 0, tiled=True)
    pieces, stream = lax.optimization_barrier((pieces, stream))
    mixed_rows = jnp.sum(pieces.astype(F32), axis=0).astype(BF)

    kv_rows, kv_part = width_kv.shape
    n_q, part = width_query.shape
    flat_kv = width_kv.reshape(kv_rows * kv_part // part, part)
    n_kv = flat_kv.shape[0]
    widths = jnp.concatenate([width_query, flat_kv, jnp.zeros_like(flat_kv)], axis=0)
    gap = widths.shape[0]
    widths = jnp.concatenate([widths, partner(widths, "x")], axis=0)
    width_own, width_other = gather_blocks(widths)

    def unflatten(start):
        own = width_own[:, start : start + n_kv]
        other = width_other[:, start : start + n_kv]
        by_distance = jnp.stack([own, other], axis=1).reshape((TS,) + own.shape[1:])
        rows = jnp.take(by_distance, t ^ jnp.arange(TS), axis=0)
        return (
            rows.reshape(TS, n_kv, kv_rows // n_kv, kv_part)
            .transpose(1, 2, 0, 3)
            .reshape(kv_rows, TS * kv_part)
        )

    wide_kv = jnp.concatenate([unflatten(0 + n_q), unflatten(gap + n_q)], axis=0)

    tokens = pair_up(hidden, "x", 0)
    token_rows = tokens.shape[0]
    streamed = dot(tokens, stream, 1, 0).astype(BF)
    streamed = streamed.reshape(token_rows, TS, -1).transpose(1, 0, 2)
    streamed = lax.all_to_all(streamed, TENSOR, 0, 0, tiled=True)
    streamed = jnp.sum(streamed.astype(F32), axis=0)
    rounded = lax.reduce_precision(streamed, 8, 7)
    streamed = jnp.concatenate([rounded, streamed - rounded], axis=0).astype(BF)
    turn = [
        ((zz * X + xx) * TS + tt, (tt * X + xx) * TS + zz)
        for zz in range(ZS)
        for xx in range(X)
        for tt in range(TS)
    ]
    streamed = lax.ppermute(streamed, SECTION + TENSOR, turn)

    near = lax.all_to_all(
        jnp.broadcast_to(mixed_rows[None], (Q,) + mixed_rows.shape), "q", 0, 0, tiled=True
    )
    of_after, of_before = shift(near, -1), shift(near, 1)
    of_far = jnp.concatenate([shift(near[..., :half], 2), shift(near[..., half:], -2)], axis=2)
    mixed = jnp.stack([near, of_after, of_far, of_before], axis=0).reshape(rows, cols)
    mixed, streamed = lax.optimization_barrier((mixed, streamed))
    streamed = lax.all_gather(streamed, Z, axis=1, tiled=True)

    wide_in, kv_in = TS * part, TS * kv_part
    expanded_query = expand_query(index, mixed, width_own, width_other, n_q, gap)
    expanded_key = dot(mixed[:, wide_in : wide_in + kv_in], wide_kv, 1, 1).astype(BF)
    expanded_value = dot(mixed[:, wide_in + kv_in :], wide_kv, 1, 1).astype(BF)
    expanded = jnp.concatenate(
        [
            expanded_query,
            expanded_key[:, :kv_rows],
            expanded_value[:, :kv_rows],
            expanded_key[:, kv_rows:],
            expanded_value[:, kv_rows:],
        ],
        axis=1,
    )
    width = expanded.shape[1]
    blocks = expanded.reshape(R, Q, deep, width)
    blocks = lax.dynamic_slice_in_dim(jnp.concatenate([blocks, blocks], 0), (R - z % R) % R, R, 0)
    expanded = blocks.transpose(1, 0, 2, 3).reshape(rows, width)
    whole = gather_tensor(expanded).reshape(TS * rows, width)

    grown_rows = stream.shape[0]
    whole_query, whole_kv = whole[:, : 2 * n_q], whole[:, 2 * n_q :]
    by_kv = dot(whole_kv, streamed, 0, 1)
    by_kv = jnp.concatenate(
        [dot(whole_kv, stream, 0, 1), by_kv[:, :token_rows] + by_kv[:, token_rows:]], axis=1
    )
    by_query = dot(streamed, whole_query, 1, 0)
    by_query = jnp.concatenate(
        [dot(stream, whole_query, 1, 0), by_query[:token_rows] + by_query[token_rows:]], axis=0
    )
    n_mine = 2 * kv_rows
    other_kv = partner(
        jnp.concatenate([by_kv[n_mine:], by_kv[:n_mine, grown_rows:]], axis=1).astype(BF), "x"
    ).astype(F32)
    other_query = partner(by_query[:, n_q:].astype(BF), "x")
    full_query = (by_query[:, :n_q] + other_query.astype(F32)).astype(BF)
    full_kv = (by_kv[:n_mine] + other_kv[:, : by_kv.shape[1]]).astype(BF)
    its_kv = (by_kv[n_mine:, grown_rows:] + other_kv[:, by_kv.shape[1] :]).astype(BF)
    grown_key = full_kv[:kv_rows, :grown_rows].T
    grown_value = full_kv[kv_rows:, :grown_rows].T

    heads_here = n_q // HD
    kv_mine = full_kv[:, grown_rows:]
    pair = jnp.stack(
        [jnp.where(x == 0, kv_mine, its_kv), jnp.where(x == 0, its_kv, kv_mine)], axis=0
    )[None]
    pair = pair_up(pair, "r", 0, 1)
    pair = pair_up(pair, "r", 0, 2)
    heads_pair = pair.reshape(R * X, 2, kv_rows, token_rows).transpose(1, 0, 2, 3)
    heads_pair = heads_pair.reshape(2 * heads_here * HD, token_rows)
    heads_pair, full_query = lax.optimization_barrier((heads_pair, full_query))
    grown_query, queries = full_query[:grown_rows], full_query[grown_rows:]
    pairs = KVH // heads_here
    route = []
    for src in range(ZS * X):
        zz, xx = src // X, src % X
        route.append((src, ((zz % R) * X + xx) * pairs + zz // R))
    kv_own, kv_other = gather_blocks(lax.ppermute(heads_pair, SECTION, route))
    attended = attend(index, queries, kv_own, kv_other)
    return (grown_query, grown_key, grown_value, attended)


def solution(mesh):
    fine = Mesh(mesh.devices.reshape(Q, R, X, Y, H, C), SECTION + TENSOR)
    placed = (
        P(SECTION, TENSOR, None),
        P(SECTION, TENSOR, None),
        P(SECTION, TENSOR, None),
        P(),
        P(SECTION, TENSOR),
        P(SECTION, TENSOR),
        P(TENSOR, SECTION),
        P(SECTION, TENSOR),
    )
    return jax.shard_map(
        per_device,
        mesh=fine,
        in_specs=placed,
        out_specs=(P(TENSOR, SECTION),) * 4,
        check_vma=False,
    )
```

time: 1040 us -> 421 us (0.40)
  the two profiles are of different devices: /device:TPU:1 before, /device:TPU:167 now
where the time goes in v1:
time: 421 us; the launch traced here: 419 us
  waiting for transfers between devices  208 us (49%)
  starting transfers between devices  148 us (35%)
  other arithmetic  18.6 us (4%)
  between operations  15.1 us (4%)
  local copies, waits for them, and re-layouts  14.5 us (3%)
  matrix products  9.95 us (2%)
  Pallas kernels  5.08 us (1%)
    ppermute x19, waiting for transfers between devices, partner(): return lax.ppermute(value, axis, [(i, i ^ bit) for i in range(size)])  84.9 us
    ppermute x19, starting transfers between devices, partner(): return lax.ppermute(value, axis, [(i, i ^ bit) for i in range(size)])  79.2 us
    all_gather x1, waiting for transfers between devices, per_device(): streamed = lax.all_gather(streamed, Z, axis=1, tiled=True)  49.9 us
    ppermute x8, starting transfers between devices, shift(): return lax.ppermute(value, Z, [(i, (i + distance) % ZS) for i in range(ZS)])  28.2 us
    all_to_all x1, waiting for transfers between devices, per_device(): lax.all_to_all(jnp.broadcast_to(mixed_rows[None], (Q,) + mixed_rows.shape...  19.5 us
    all_to_all x1, waiting for transfers between devices, per_device(): pieces = lax.all_to_all(summed, 'q', 0, 0, tiled=True)  17.5 us
    all_to_all x1, starting transfers between devices, per_device(): streamed = lax.all_to_all(streamed, TENSOR, 0, 0, tiled=True)  16.6 us
    ppermute x1, waiting for transfers between devices, per_device(): kv_own, kv_other = gather_blocks(lax.ppermute(heads_pair, SECTION, route))  15.2 us
  transfers between devices with their start and end apart: 34, of which 21 were waited for; matrix products, arithmetic and copies ran while one was open for 7% of the time, Pallas kernels for 0%

profile of v1, /device:TPU:167, one launch (start us, length us, event | category | flops | bytes accessed | tf_op | source)
XLA Modules:
  0.0 418.9 jit_solution(2694579461670686061)
XLA Ops:
  15.4 3.5 collective-permute-start
  26.7 5.5 %collective-permute-start.2 = (bf16[2,4,8,3072]{3,2,1,0:T(8,128)(2,1)}, bf16[2,4,8,3072]{3,2,1,0:T(8,128)(2,1)}, u32[]{:S(2)}, u32[]{:S(2)}) collective-permute-start(bf16[2,4,8,3072]{3,2,1,0:T(8,128)(2,1)} %get-tuple-element.43), channel_id=1, source_target_pairs={{0,64},{32,96},{64,128},{96,160},{128,192},{160,224},{192,256},{22... | collective-permute-start | bytes 1179656 | tf_op jit(solution)/shard_map/ppermute | solution.py:22
  38.1 3.7 fusion.4
  41.9 7.3 %collective-permute-done.13 = bf16[2,544,256]{2,1,0:T(8,128)(2,1)S(1)} collective-permute-done((bf16[2,544,256]{2,1,0:T(8,128)(2,1)S(1)}, bf16[2,544,256]{2,1,0:T(8,128)(2,1)S(1)}, u32[]{:S(2)}, u32[]{:S(2)}) %collective-permute-start.13) | collective-permute-done | bytes 557088 | tf_op jit(solution)/shard_map/ppermute | solution.py:27
  49.3 4.8 %collective-permute-start.14 = (bf16[2,2,544,256]{3,2,1,0:T(8,128)(2,1)S(1)}, bf16[2,2,544,256]{3,2,1,0:T(8,128)(2,1)S(1)}, u32[]{:S(2)}, u32[]{:S(2)}) collective-permute-start(bf16[2,2,544,256]{3,2,1,0:T(8,128)(2,1)S(1)} %get-tuple-element.41), channel_id=1, source_target_pairs={{0,8},{4,12},{8,0},{12,4},{1,9},{5,13},{9,1},{13,5},{2,10},{6,14},... | collective-permute-start | bytes 3342344 | tf_op jit(solution)/shard_map/ppermute | solution.py:27
  60.9 15.2 %collective-permute-done.14 = bf16[2,2,544,256]{3,2,1,0:T(8,128)(2,1)S(1)} collective-permute-done((bf16[2,2,544,256]{3,2,1,0:T(8,128)(2,1)S(1)}, bf16[2,2,544,256]{3,2,1,0:T(8,128)(2,1)S(1)}, u32[]{:S(2)}, u32[]{:S(2)}) %collective-permute-start.14) | collective-permute-done | bytes 1114144 | tf_op jit(solution)/shard_map/ppermute | solution.py:27
  78.6 5.7 %collective-permute-start.15 = (bf16[8,544,256]{2,1,0:T(8,128)(2,1)S(1)}, bf16[8,544,256]{2,1,0:T(8,128)(2,1)}, u32[]{:S(2)}, u32[]{:S(2)}) collective-permute-start(bf16[8,544,256]{2,1,0:T(8,128)(2,1)S(1)} %bitcast.124), channel_id=1, source_target_pairs={{0,1},{1,0},{2,3},{3,2},{4,5},{5,4},{6,7},{7,6},{8,9},{9,8},{10,11... | collective-permute-start | bytes 6684680 | tf_op jit(solution)/shard_map/ppermute | solution.py:27
  86.2 10.0 %all-to-all-start = ((bf16[4,8,6144]{2,1,0:T(8,128)(2,1)}), bf16[4,8,6144]{2,1,0:T(8,128)(2,1)S(1)}, u32[]{:S(2)}, u32[]{:S(2)}) async-start(bf16[4,8,6144]{2,1,0:T(8,128)(2,1)} %fusion.8), calls=%async_computation | async-start | bytes 786432 | tf_op jit(solution)/shard_map/all_to_all | solution.py:179
  101.5 17.5 %all-to-all-done = bf16[4,8,6144]{2,1,0:T(8,128)(2,1)S(1)} async-done(((bf16[4,8,6144]{2,1,0:T(8,128)(2,1)}), bf16[4,8,6144]{2,1,0:T(8,128)(2,1)S(1)}, u32[]{:S(2)}, u32[]{:S(2)}) %all-to-all-start) | async-done | bytes 393248 | tf_op jit(solution)/shard_map/all_to_all | solution.py:179
  122.0 16.6 %all-to-all-start.2 = ((bf16[16,128,128]{2,1,0:T(8,128)(2,1)}), bf16[16,128,128]{2,1,0:T(8,128)(2,1)S(1)}, u32[]{:S(2)}, u32[]{:S(2)}) async-start(bf16[16,128,128]{2,1,0:T(8,128)(2,1)} %bitcast.140), calls=%async_computation.2 | async-start | bytes 1048576 | tf_op jit(solution)/shard_map/all_to_all | solution.py:209
  138.7 9.6 %all-to-all-done.2 = bf16[16,128,128]{2,1,0:T(8,128)(2,1)S(1)} async-done(((bf16[16,128,128]{2,1,0:T(8,128)(2,1)}), bf16[16,128,128]{2,1,0:T(8,128)(2,1)S(1)}, u32[]{:S(2)}, u32[]{:S(2)}) %all-to-all-start.2) | async-done | bytes 524320 | tf_op jit(solution)/shard_map/all_to_all | solution.py:209
  149.1 7.6 %all-to-all-start.1 = ((bf16[4,8,6144]{2,1,0:T(8,128)(2,1)}), bf16[4,8,6144]{2,1,0:T(8,128)(2,1)S(1)}, u32[]{:S(2)}, u32[]{:S(2)}) async-start(bf16[4,8,6144]{2,1,0:T(8,128)(2,1)} %broadcast_in_dim.31), calls=%async_computation.1 | async-start | bytes 786432 | tf_op jit(solution)/shard_map/all_to_all | solution.py:221
  159.6 19.5 %all-to-all-done.1 = bf16[4,8,6144]{2,1,0:T(8,128)(2,1)S(1)} async-done(((bf16[4,8,6144]{2,1,0:T(8,128)(2,1)}), bf16[4,8,6144]{2,1,0:T(8,128)(2,1)S(1)}, u32[]{:S(2)}, u32[]{:S(2)}) %all-to-all-start.1) | async-done | bytes 393248 | tf_op jit(solution)/shard_map/all_to_all | solution.py:221
  181.0 4.3 %collective-permute-start.6 = (bf16[4,8,3072]{2,1,0:T(8,128)(2,1)S(1)}, bf16[4,8,3072]{2,1,0:T(8,128)(2,1)S(1)}, u32[]{:S(2)}, u32[]{:S(2)}) collective-permute-start(bf16[4,8,3072]{2,1,0:T(8,128)(2,1)S(1)} %get-tuple-element.50), channel_id=1, source_target_pairs={{0,64},{32,96},{64,128},{96,160},{128,192},{160,224},{192,256},{22... | collective-permute-start | bytes 589832 | tf_op jit(solution)/shard_map/ppermute | solution.py:22
  185.3 4.0 collective-permute-start.10
  189.4 5.9 %collective-permute-start.8 = (bf16[4,8,6144]{2,1,0:T(8,128)(2,1)S(1)}, bf16[4,8,6144]{2,1,0:T(8,128)(2,1)S(1)}, u32[]{:S(2)}, u32[]{:S(2)}) collective-permute-start(bf16[4,8,6144]{2,1,0:T(8,128)(2,1)S(1)} %all-to-all-done.1), channel_id=1, source_target_pairs={{0,32},{32,64},{64,96},{96,128},{128,160},{160,192},{192,224},{224... | collective-permute-start | bytes 1179656 | tf_op jit(solution)/shard_map/ppermute | solution.py:22
  198.0 6.8 %collective-permute-done.8 = bf16[4,8,6144]{2,1,0:T(8,128)(2,1)S(1)} collective-permute-done((bf16[4,8,6144]{2,1,0:T(8,128)(2,1)S(1)}, bf16[4,8,6144]{2,1,0:T(8,128)(2,1)S(1)}, u32[]{:S(2)}, u32[]{:S(2)}) %collective-permute-start.8) | collective-permute-done | bytes 393248 | tf_op jit(solution)/shard_map/ppermute | solution.py:22
  204.8 4.4 %collective-permute-done.5 = bf16[4,8,6144]{2,1,0:T(8,128)(2,1)S(1)} collective-permute-done((bf16[4,8,6144]{2,1,0:T(8,128)(2,1)S(1)}, bf16[4,8,6144]{2,1,0:T(8,128)(2,1)S(1)}, u32[]{:S(2)}, u32[]{:S(2)}) %collective-permute-start.5) | collective-permute-done | bytes 393248 | tf_op jit(solution)/shard_map/ppermute | solution.py:22
  219.8 7.2 %collective-permute-done.16 = bf16[1,128,640]{2,1,0:T(8,128)(2,1)S(1)} collective-permute-done((bf16[1,128,640]{2,1,0:T(8,128)(2,1)S(1)}, bf16[1,128,640]{2,1,0:T(8,128)(2,1)S(1)}, u32[]{:S(2)}, u32[]{:S(2)}) %collective-permute-start.16) | collective-permute-done | bytes 163872 | tf_op jit(solution)/shard_map/ppermute | solution.py:27
  229.0 8.3 %collective-permute-done.17 = bf16[1,2,128,640]{3,2,1,0:T(8,128)(2,1)S(1)} collective-permute-done((bf16[1,2,128,640]{3,2,1,0:T(8,128)(2,1)S(1)}, bf16[1,2,128,640]{3,2,1,0:T(8,128)(2,1)S(1)}, u32[]{:S(2)}, u32[]{:S(2)}) %collective-permute-start.17) | collective-permute-done | bytes 327712 | tf_op jit(solution)/shard_map/ppermute | solution.py:27
  239.4 15.9 %collective-permute-done.18 = bf16[1,2,2,128,640]{4,3,2,1,0:T(8,128)(2,1)S(1)} collective-permute-done((bf16[1,2,2,128,640]{4,3,2,1,0:T(8,128)(2,1)S(1)}, bf16[1,2,2,128,640]{4,3,2,1,0:T(8,128)(2,1)S(1)}, u32[]{:S(2)}, u32[]{:S(2)}) %collective-permute-start.18) | collective-permute-done | bytes 655392 | tf_op jit(solution)/shard_map/ppermute | solution.py:27
  255.7 4.6 %collective-permute-start.19 = (bf16[8,1,128,640]{3,2,1,0:T(8,128)(2,1)S(1)}, bf16[8,1,128,640]{3,2,1,0:T(8,128)(2,1)S(1)}, u32[]{:S(2)}, u32[]{:S(2)}) collective-permute-start(bf16[8,1,128,640]{3,2,1,0:T(8,128)(2,1)S(1)} %bitcast.132), channel_id=1, source_target_pairs={{0,1},{1,0},{2,3},{3,2},{4,5},{5,4},{6,7},{7,6},{8,9},{9,8},{10,11... | collective-permute-start | bytes 3932168 | tf_op jit(solution)/shard_map/ppermute | solution.py:27
  267.8 49.9 %all-gather.5.cloned.1.call-done = bf16[256,2048]{1,0:T(8,128)(2,1)} async-done(((bf16[256,128]{1,0:T(8,128)(2,1)}), bf16[256,2048]{1,0:T(8,128)(2,1)}) %all-gather.5.cloned.1.call-update) | async-done | bytes 1048592 | tf_op jit(solution)/shard_map/all_gather | solution.py:228
  329.8 3.5 collective-permute-start.22
  335.9 5.3 %collective-permute-done.23 = bf16[640,256]{1,0:T(8,128)(2,1)S(1)} collective-permute-done((bf16[640,256]{1,0:T(8,128)(2,1)S(1)}, bf16[640,256]{1,0:T(8,128)(2,1)S(1)}, u32[]{:S(2)}, u32[]{:S(2)}) %collective-permute-start.23) | collective-permute-done | bytes 327712 | tf_op jit(solution)/shard_map/ppermute | solution.py:27
  343.4 15.2 %collective-permute-done.24 = bf16[512,128]{1,0:T(8,128)(2,1)S(1)} collective-permute-done((bf16[512,128]{1,0:T(8,128)(2,1)S(1)}, bf16[512,128]{1,0:T(8,128)(2,1)S(1)}, u32[]{:S(2)}, u32[]{:S(2)}) %collective-permute-start.24) | collective-permute-done | bytes 131104 | tf_op jit(solution)/shard_map/ppermute | solution.py:287
  358.5 3.3 collective-permute-start.25
  361.8 3.9 collective-permute-done.25
  368.9 4.3 %collective-permute-done.26 = bf16[2,512,128]{2,1,0:T(8,128)(2,1)S(1)} collective-permute-done((bf16[2,512,128]{2,1,0:T(8,128)(2,1)S(1)}, bf16[2,512,128]{2,1,0:T(8,128)(2,1)S(1)}, u32[]{:S(2)}, u32[]{:S(2)}) %collective-permute-start.26) | collective-permute-done | bytes 262176 | tf_op jit(solution)/shard_map/ppermute | solution.py:27
  373.3 4.6 %collective-permute-start.27 = (bf16[2,2,512,128]{3,2,1,0:T(8,128)(2,1)S(1)}, bf16[2,2,512,128]{3,2,1,0:T(8,128)(2,1)S(1)}, u32[]{:S(2)}, u32[]{:S(2)}) collective-permute-start(bf16[2,2,512,128]{3,2,1,0:T(8,128)(2,1)S(1)} %get-tuple-element.49), channel_id=1, source_target_pairs={{0,8},{4,12},{8,0},{12,4},{1,9},{5,13},{9,1},{13,5},{2,10},{6,14},... | collective-permute-start | bytes 1572872 | tf_op jit(solution)/shard_map/ppermute | solution.py:27
  377.9 6.8 %collective-permute-done.27 = bf16[2,2,512,128]{3,2,1,0:T(8,128)(2,1)S(1)} collective-permute-done((bf16[2,2,512,128]{3,2,1,0:T(8,128)(2,1)S(1)}, bf16[2,2,512,128]{3,2,1,0:T(8,128)(2,1)S(1)}, u32[]{:S(2)}, u32[]{:S(2)}) %collective-permute-start.27) | collective-permute-done | bytes 524320 | tf_op jit(solution)/shard_map/ppermute | solution.py:27
  384.8 22.9 %collective-permute-start.28 = (bf16[8,512,128]{2,1,0:T(8,128)(2,1)S(1)}, bf16[8,512,128]{2,1,0:T(8,128)(2,1)S(1)}, u32[]{:S(2)}, u32[]{:S(2)}) collective-permute-start(bf16[8,512,128]{2,1,0:T(8,128)(2,1)S(1)} %bitcast.130), channel_id=1, source_target_pairs={{0,1},{1,0},{2,3},{3,2},{4,5},{5,4},{6,7},{7,6},{8,9},{9,8},{10,11... | collective-permute-start | bytes 3145736 | tf_op jit(solution)/shard_map/ppermute | solution.py:27
  (157 shorter events, 96.1 us)
Async XLA Ops:
  7.2 111.9 %all-gather.3.cloned.1.call-start = ((), (), s32[]{:S(2)}) async-start(), calls=%async_computation.3 | async-start | bytes 2228224 | tf_op jit(solution)/shard_map/all_gather | solution.py:145
  10.9 8.1 %collective-permute-start.11 = (bf16[272,256]{1,0:T(8,128)(2,1)S(1)}, bf16[272,256]{1,0:T(8,128)(2,1)S(1)}, u32[]{:S(2)}, u32[]{:S(2)}) collective-permute-start(bf16[272,256]{1,0:T(8,128)(2,1)S(1)} %pad_maximum_fusion.13), channel_id=1, source_target_pairs={{0,16},{16,0},{1,17},{17,1},{2,18},{18,2},{3,19},{19,3},{4,20},{20... | collective-permute-start | bytes 417800 | tf_op jit(solution)/shard_map/ppermute | solution.py:27
  13.5 24.6 %collective-permute-start.1 = (bf16[2,4,8,6144]{3,2,1,0:T(8,128)(2,1)}, bf16[2,4,8,6144]{3,2,1,0:T(8,128)(2,1)}, u32[]{:S(2)}, u32[]{:S(2)}) collective-permute-start(bf16[2,4,8,6144]{3,2,1,0:T(8,128)(2,1)} %get-tuple-element.16), channel_id=1, source_target_pairs={{0,480},{32,0},{64,32},{96,64},{128,96},{160,128},{192,160},{224,1... | collective-permute-start | bytes 2359304 | tf_op jit(solution)/shard_map/ppermute | solution.py:22
  15.4 22.7 %collective-permute-start = (bf16[2,4,8,6144]{3,2,1,0:T(8,128)(2,1)}, bf16[2,4,8,6144]{3,2,1,0:T(8,128)(2,1)}, u32[]{:S(2)}, u32[]{:S(2)}) collective-permute-start(bf16[2,4,8,6144]{3,2,1,0:T(8,128)(2,1)} %get-tuple-element.15), channel_id=1, source_target_pairs={{0,32},{32,64},{64,96},{96,128},{128,160},{160,192},{192,224},{224... | collective-permute-start | bytes 2359304 | tf_op jit(solution)/shard_map/ppermute | solution.py:22
  20.5 13.4 %collective-permute-start.12 = (bf16[544,256]{1,0:T(8,128)(2,1)}, bf16[544,256]{1,0:T(8,128)(2,1)}, u32[]{:S(2)}, u32[]{:S(2)}) collective-permute-start(bf16[544,256]{1,0:T(8,128)(2,1)} %get-tuple-element.55), channel_id=1, source_target_pairs={{0,2},{2,0},{1,3},{3,1},{4,6},{6,4},{5,7},{7,5},{8,10},{10,8},{9,1... | collective-permute-start | bytes 835592 | tf_op jit(solution)/shard_map/ppermute | solution.py:27
  24.2 29.9 %collective-permute-start.3 = (bf16[2,4,8,3072]{3,2,1,0:T(8,128)(2,1)}, bf16[2,4,8,3072]{3,2,1,0:T(8,128)(2,1)}, u32[]{:S(2)}, u32[]{:S(2)}) collective-permute-start(bf16[2,4,8,3072]{3,2,1,0:T(8,128)(2,1)} %get-tuple-element.42), channel_id=1, source_target_pairs={{0,448},{32,480},{64,0},{96,32},{128,64},{160,96},{192,128},{224,1... | collective-permute-start | bytes 1179656 | tf_op jit(solution)/shard_map/ppermute | solution.py:22
  26.7 27.5 %collective-permute-start.2 = (bf16[2,4,8,3072]{3,2,1,0:T(8,128)(2,1)}, bf16[2,4,8,3072]{3,2,1,0:T(8,128)(2,1)}, u32[]{:S(2)}, u32[]{:S(2)}) collective-permute-start(bf16[2,4,8,3072]{3,2,1,0:T(8,128)(2,1)} %get-tuple-element.43), channel_id=1, source_target_pairs={{0,64},{32,96},{64,128},{96,160},{128,192},{160,224},{192,256},{22... | collective-permute-start | bytes 1179656 | tf_op jit(solution)/shard_map/ppermute | solution.py:22
  34.9 14.2 %collective-permute-start.13 = (bf16[2,544,256]{2,1,0:T(8,128)(2,1)S(1)}, bf16[2,544,256]{2,1,0:T(8,128)(2,1)S(1)}, u32[]{:S(2)}, u32[]{:S(2)}) collective-permute-start(bf16[2,544,256]{2,1,0:T(8,128)(2,1)S(1)} %get-tuple-element.47), channel_id=1, source_target_pairs={{0,4},{4,0},{8,12},{12,8},{1,5},{5,1},{9,13},{13,9},{2,6},{6,2},{1... | collective-permute-start | bytes 1671176 | tf_op jit(solution)/shard_map/ppermute | solution.py:27
  49.3 26.7 %collective-permute-start.14 = (bf16[2,2,544,256]{3,2,1,0:T(8,128)(2,1)S(1)}, bf16[2,2,544,256]{3,2,1,0:T(8,128)(2,1)S(1)}, u32[]{:S(2)}, u32[]{:S(2)}) collective-permute-start(bf16[2,2,544,256]{3,2,1,0:T(8,128)(2,1)S(1)} %get-tuple-element.41), channel_id=1, source_target_pairs={{0,8},{4,12},{8,0},{12,4},{1,9},{5,13},{9,1},{13,5},{2,10},{6,14},... | collective-permute-start | bytes 3342344 | tf_op jit(solution)/shard_map/ppermute | solution.py:27
  58.4 25.9 %collective-permute-start.4 = (bf16[4,8,6144]{2,1,0:T(8,128)(2,1)}, bf16[4,8,6144]{2,1,0:T(8,128)(2,1)}, u32[]{:S(2)}, u32[]{:S(2)}) collective-permute-start(bf16[4,8,6144]{2,1,0:T(8,128)(2,1)} %fusion.18), channel_id=1, source_target_pairs={{0,16},{16,0},{1,17},{17,1},{2,18},{18,2},{3,19},{19,3},{4,20},{20... | collective-permute-start | bytes 1179656 | tf_op jit(solution)/shard_map/ppermute | solution.py:27
  78.6 78.1 %collective-permute-start.15 = (bf16[8,544,256]{2,1,0:T(8,128)(2,1)S(1)}, bf16[8,544,256]{2,1,0:T(8,128)(2,1)}, u32[]{:S(2)}, u32[]{:S(2)}) collective-permute-start(bf16[8,544,256]{2,1,0:T(8,128)(2,1)S(1)} %bitcast.124), channel_id=1, source_target_pairs={{0,1},{1,0},{2,3},{3,2},{4,5},{5,4},{6,7},{7,6},{8,9},{9,8},{10,11... | collective-permute-start | bytes 6684680 | tf_op jit(solution)/shard_map/ppermute | solution.py:27
  86.2 32.9 %all-to-all-start = ((bf16[4,8,6144]{2,1,0:T(8,128)(2,1)}), bf16[4,8,6144]{2,1,0:T(8,128)(2,1)S(1)}, u32[]{:S(2)}, u32[]{:S(2)}) async-start(bf16[4,8,6144]{2,1,0:T(8,128)(2,1)} %fusion.8), calls=%async_computation | async-start | bytes 786432 | tf_op jit(solution)/shard_map/all_to_all | solution.py:179
  122.0 26.3 %all-to-all-start.2 = ((bf16[16,128,128]{2,1,0:T(8,128)(2,1)}), bf16[16,128,128]{2,1,0:T(8,128)(2,1)S(1)}, u32[]{:S(2)}, u32[]{:S(2)}) async-start(bf16[16,128,128]{2,1,0:T(8,128)(2,1)} %bitcast.140), calls=%async_computation.2 | async-start | bytes 1048576 | tf_op jit(solution)/shard_map/all_to_all | solution.py:209
  149.1 29.9 %all-to-all-start.1 = ((bf16[4,8,6144]{2,1,0:T(8,128)(2,1)}), bf16[4,8,6144]{2,1,0:T(8,128)(2,1)S(1)}, u32[]{:S(2)}, u32[]{:S(2)}) async-start(bf16[4,8,6144]{2,1,0:T(8,128)(2,1)} %broadcast_in_dim.31), calls=%async_computation.1 | async-start | bytes 786432 | tf_op jit(solution)/shard_map/all_to_all | solution.py:221
  156.7 161.1 %all-gather.5.cloned.1.call-start = ((), (), s32[]{:S(2)}) async-start(), calls=%async_computation.4 | async-start | bytes 1114112 | tf_op jit(solution)/shard_map/all_gather | solution.py:228
  179.1 18.9 %collective-permute-start.7 = (bf16[4,8,3072]{2,1,0:T(8,128)(2,1)S(1)}, bf16[4,8,3072]{2,1,0:T(8,128)(2,1)S(1)}, u32[]{:S(2)}, u32[]{:S(2)}) collective-permute-start(bf16[4,8,3072]{2,1,0:T(8,128)(2,1)S(1)} %get-tuple-element.51), channel_id=1, source_target_pairs={{0,448},{32,480},{64,0},{96,32},{128,64},{160,96},{192,128},{224,1... | collective-permute-start | bytes 589832 | tf_op jit(solution)/shard_map/ppermute | solution.py:22
  181.0 16.9 %collective-permute-start.6 = (bf16[4,8,3072]{2,1,0:T(8,128)(2,1)S(1)}, bf16[4,8,3072]{2,1,0:T(8,128)(2,1)S(1)}, u32[]{:S(2)}, u32[]{:S(2)}) collective-permute-start(bf16[4,8,3072]{2,1,0:T(8,128)(2,1)S(1)} %get-tuple-element.50), channel_id=1, source_target_pairs={{0,64},{32,96},{64,128},{96,160},{128,192},{160,224},{192,256},{22... | collective-permute-start | bytes 589832 | tf_op jit(solution)/shard_map/ppermute | solution.py:22
  185.3 25.3 %collective-permute-start.10 = (bf16[256,128]{1,0:T(8,128)(2,1)S(1)}, bf16[256,128]{1,0:T(8,128)(2,1)S(1)}, u32[]{:S(2)}, u32[]{:S(2)}) collective-permute-start(bf16[256,128]{1,0:T(8,128)(2,1)S(1)} %pad_maximum_fusion.16), channel_id=1, source_target_pairs={{0,0},{1,32},{2,64},{3,96},{4,128},{5,160},{6,192},{7,224},{8,256}... | collective-permute-start | bytes 196616 | tf_op jit(solution)/shard_map/ppermute | solution.py:219
  189.4 15.5 %collective-permute-start.8 = (bf16[4,8,6144]{2,1,0:T(8,128)(2,1)S(1)}, bf16[4,8,6144]{2,1,0:T(8,128)(2,1)S(1)}, u32[]{:S(2)}, u32[]{:S(2)}) collective-permute-start(bf16[4,8,6144]{2,1,0:T(8,128)(2,1)S(1)} %all-to-all-done.1), channel_id=1, source_target_pairs={{0,32},{32,64},{64,96},{96,128},{128,160},{160,192},{192,224},{224... | collective-permute-start | bytes 1179656 | tf_op jit(solution)/shard_map/ppermute | solution.py:22
  195.2 14.0 %collective-permute-start.5 = (bf16[4,8,6144]{2,1,0:T(8,128)(2,1)S(1)}, bf16[4,8,6144]{2,1,0:T(8,128)(2,1)S(1)}, u32[]{:S(2)}, u32[]{:S(2)}) collective-permute-start(bf16[4,8,6144]{2,1,0:T(8,128)(2,1)S(1)} %all-to-all-done.1), channel_id=1, source_target_pairs={{0,480},{32,0},{64,32},{96,64},{128,96},{160,128},{192,160},{224,1... | collective-permute-start | bytes 1179656 | tf_op jit(solution)/shard_map/ppermute | solution.py:22
  217.8 9.2 %collective-permute-start.16 = (bf16[1,128,640]{2,1,0:T(8,128)(2,1)S(1)}, bf16[1,128,640]{2,1,0:T(8,128)(2,1)S(1)}, u32[]{:S(2)}, u32[]{:S(2)}) collective-permute-start(bf16[1,128,640]{2,1,0:T(8,128)(2,1)S(1)} %bitcast.143), channel_id=1, source_target_pairs={{0,2},{2,0},{1,3},{3,1},{4,6},{6,4},{5,7},{7,5},{8,10},{10,8},{9,1... | collective-permute-start | bytes 491528 | tf_op jit(solution)/shard_map/ppermute | solution.py:27
  227.1 10.2 %collective-permute-start.17 = (bf16[1,2,128,640]{3,2,1,0:T(8,128)(2,1)S(1)}, bf16[1,2,128,640]{3,2,1,0:T(8,128)(2,1)S(1)}, u32[]{:S(2)}, u32[]{:S(2)}) collective-permute-start(bf16[1,2,128,640]{3,2,1,0:T(8,128)(2,1)S(1)} %maximum_bitcast_fusion.2), channel_id=1, source_target_pairs={{0,4},{4,0},{8,12},{12,8},{1,5},{5,1},{9,13},{13,9},{2,6},{6,2},{1... | collective-permute-start | bytes 983048 | tf_op jit(solution)/shard_map/ppermute | solution.py:27
  237.5 17.9 %collective-permute-start.18 = (bf16[1,2,2,128,640]{4,3,2,1,0:T(8,128)(2,1)S(1)}, bf16[1,2,2,128,640]{4,3,2,1,0:T(8,128)(2,1)S(1)}, u32[]{:S(2)}, u32[]{:S(2)}) collective-permute-start(bf16[1,2,2,128,640]{4,3,2,1,0:T(8,128)(2,1)S(1)} %maximum_bitcast_fusion), channel_id=1, source_target_pairs={{0,8},{4,12},{8,0},{12,4},{1,9},{5,13},{9,1},{13,5},{2,10},{6,14},... | collective-permute-start | bytes 1966088 | tf_op jit(solution)/shard_map/ppermute | solution.py:27
  255.7 7.2 %collective-permute-start.19 = (bf16[8,1,128,640]{3,2,1,0:T(8,128)(2,1)S(1)}, bf16[8,1,128,640]{3,2,1,0:T(8,128)(2,1)S(1)}, u32[]{:S(2)}, u32[]{:S(2)}) collective-permute-start(bf16[8,1,128,640]{3,2,1,0:T(8,128)(2,1)S(1)} %bitcast.132), channel_id=1, source_target_pairs={{0,1},{1,0},{2,3},{3,2},{4,5},{5,4},{6,7},{7,6},{8,9},{9,8},{10,11... | collective-permute-start | bytes 3932168 | tf_op jit(solution)/shard_map/ppermute | solution.py:27
  319.6 5.4 %collective-permute-start.20 = (bf16[64,768]{1,0:T(8,128)(2,1)S(1)}, bf16[64,768]{1,0:T(8,128)(2,1)S(1)}, u32[]{:S(2)}, u32[]{:S(2)}) collective-permute-start(bf16[64,768]{1,0:T(8,128)(2,1)S(1)} %pad_maximum_fusion.15), channel_id=1, source_target_pairs={{0,16},{16,0},{1,17},{17,1},{2,18},{18,2},{3,19},{19,3},{4,20},{20... | collective-permute-start | bytes 294920 | tf_op jit(solution)/shard_map/ppermute | solution.py:27
  329.8 6.0 %collective-permute-start.22 = (bf16[2,2,64,128]{3,2,1,0:T(8,128)(2,1)S(1)}, bf16[2,2,64,128]{3,2,1,0:T(8,128)(2,1)S(1)}, u32[]{:S(2)}, u32[]{:S(2)}) collective-permute-start(bf16[2,2,64,128]{3,2,1,0:T(8,128)(2,1)S(1)} %pad_maximum_fusion.19), channel_id=1, source_target_pairs={{0,64},{32,96},{64,0},{96,32},{1,65},{33,97},{65,1},{97,33},{2,66}... | collective-permute-start | bytes 196616 | tf_op jit(solution)/shard_map/ppermute | solution.py:27
  333.4 7.8 %collective-permute-start.23 = (bf16[640,256]{1,0:T(8,128)(2,1)S(1)}, bf16[640,256]{1,0:T(8,128)(2,1)S(1)}, u32[]{:S(2)}, u32[]{:S(2)}) collective-permute-start(bf16[640,256]{1,0:T(8,128)(2,1)S(1)} %fusion.12), channel_id=1, source_target_pairs={{0,16},{16,0},{1,17},{17,1},{2,18},{18,2},{3,19},{19,3},{4,20},{20... | collective-permute-start | bytes 983048 | tf_op jit(solution)/shard_map/ppermute | solution.py:27
  341.3 17.2 %collective-permute-start.24 = (bf16[512,128]{1,0:T(8,128)(2,1)S(1)}, bf16[512,128]{1,0:T(8,128)(2,1)S(1)}, u32[]{:S(2)}, u32[]{:S(2)}) collective-permute-start(bf16[512,128]{1,0:T(8,128)(2,1)S(1)} %bitcast.157), channel_id=1, source_target_pairs={{0,0},{16,64},{32,128},{48,192},{64,256},{80,320},{96,384},{112,44... | collective-permute-start | bytes 393224 | tf_op jit(solution)/shard_map/ppermute | solution.py:287
  358.5 7.2 %collective-permute-start.25 = (bf16[512,128]{1,0:T(8,128)(2,1)S(1)}, bf16[512,128]{1,0:T(8,128)(2,1)S(1)}, u32[]{:S(2)}, u32[]{:S(2)}) collective-permute-start(bf16[512,128]{1,0:T(8,128)(2,1)S(1)} %collective-permute-done.24), channel_id=1, source_target_pairs={{0,2},{2,0},{1,3},{3,1},{4,6},{6,4},{5,7},{7,5},{8,10},{10,8},{9,1... | collective-permute-start | bytes 393224 | tf_op jit(solution)/shard_map/ppermute | solution.py:27
  365.8 7.4 %collective-permute-start.26 = (bf16[2,512,128]{2,1,0:T(8,128)(2,1)S(1)}, bf16[2,512,128]{2,1,0:T(8,128)(2,1)S(1)}, u32[]{:S(2)}, u32[]{:S(2)}) collective-permute-start(bf16[2,512,128]{2,1,0:T(8,128)(2,1)S(1)} %get-tuple-element.57), channel_id=1, source_target_pairs={{0,4},{4,0},{8,12},{12,8},{1,5},{5,1},{9,13},{13,9},{2,6},{6,2},{1... | collective-permute-start | bytes 786440 | tf_op jit(solution)/shard_map/ppermute | solution.py:27
  373.3 11.4 %collective-permute-start.27 = (bf16[2,2,512,128]{3,2,1,0:T(8,128)(2,1)S(1)}, bf16[2,2,512,128]{3,2,1,0:T(8,128)(2,1)S(1)}, u32[]{:S(2)}, u32[]{:S(2)}) collective-permute-start(bf16[2,2,512,128]{3,2,1,0:T(8,128)(2,1)S(1)} %get-tuple-element.49), channel_id=1, source_target_pairs={{0,8},{4,12},{8,0},{12,4},{1,9},{5,13},{9,1},{13,5},{2,10},{6,14},... | collective-permute-start | bytes 1572872 | tf_op jit(solution)/shard_map/ppermute | solution.py:27
  384.8 25.2 %collective-permute-start.28 = (bf16[8,512,128]{2,1,0:T(8,128)(2,1)S(1)}, bf16[8,512,128]{2,1,0:T(8,128)(2,1)S(1)}, u32[]{:S(2)}, u32[]{:S(2)}) collective-permute-start(bf16[8,512,128]{2,1,0:T(8,128)(2,1)S(1)} %bitcast.130), channel_id=1, source_target_pairs={{0,1},{1,0},{2,3},{3,2},{4,5},{5,4},{6,7},{7,6},{8,9},{9,8},{10,11... | collective-permute-start | bytes 3145736 | tf_op jit(solution)/shard_map/ppermute | solution.py:27
  (17 other events, 93.7 us)
Sparse Core Ops, SparseCore 0:
  32.3 84.5 all-gather.2
  260.4 57.3 all-gather.4
